TPU v7x, 1024 devices: a whole 4x4x32 slice. The times are simulated.
1024 devices in a mesh: box: 4 (over x_hi, core), dir: 256 (over y, x_lo, z).
Axes of the slice: x: 4 (x_hi: 2, x_lo: 2; x = x_hi * 2 + x_lo), y: 4, z: 32, core: 2. Of those that a mesh axis runs over, the one named last changes fastest.
Arguments:
- patterns: float32 [4, 2048, 64, 256], P('box', 'dir'), may hold values from -4 to 4
- far_boxes: int32 [256, 32, 16], P('dir'), may hold values from 0 to 31
- far_types: int32 [256, 32, 16], P('dir'), may hold values from 0 to 315
- transfer: bfloat16 [316, 64, 256], P(None, 'box'), may hold values from -1.5 to 1.5
Outputs:
- incoming: float32 [256, 32, 64, 256], P('dir', None, 'box')
- aggregated: float32 [1024, 128, 512], P('dir', 'box')
All inputs are finite; a program needn't handle non-finite values.
Results may differ from a plain program's by a relative error of at most 0.0003.
Values sent between devices are 32-bit elements; how exact they have to be, the bound alone decides.
A program may use at most 64 MiB of HBM per device.

v0:
```python
import math

import jax
import jax.numpy as jnp
from jax import lax
from jax.sharding import PartitionSpec as P

TH = 64
LEVELS = 3


two_pi = 2.0 * math.pi
step_phase = 8.0
outer_weight = -0.0390625
inner_weight = 0.2734375
center_weight = 0.8203125
across_weight = -0.0546875


def swapped(block, axis, stride):
    count = lax.axis_size(axis)
    route = []
    for low in range(count):
        high = low | 1 << stride
        if high != low and high < count:
            route += [(low, high), (high, low)]
    return lax.ppermute(block, axis, route)


def extended_2(value, sides, width):
    for axis, dim in sides:
        size, length = (lax.axis_size(axis), value.shape[dim])
        up = [(i, (i + 1) % size) for i in range(size - 1)]
        down = [(j, i) for i, j in up]
        last = lax.slice_in_dim(value, length - width, length, axis=dim)
        leading = lax.slice_in_dim(value, 0, width, axis=dim)
        before = lax.ppermute(last, axis, up)
        after = lax.ppermute(leading, axis, down)
        value = jnp.concatenate([before, value, after], axis=dim)
    return value


def interp_table(azimuth):
    orders = jnp.arange(azimuth // 2 + 1, dtype=jnp.int32)
    source_index = jnp.arange(azimuth, dtype=jnp.int32)
    target_index = jnp.arange(2 * azimuth, dtype=jnp.int32)
    source_angle = (
        two_pi / azimuth * (orders[:, None] * source_index[None, :] % azimuth).astype(jnp.float32)
    )
    target_angle = (
        two_pi
        / (2 * azimuth)
        * (orders[:, None] * target_index[None, :] % (2 * azimuth)).astype(jnp.float32)
    )
    weights = (
        jnp.where((orders == 0) | (orders == azimuth // 2), 1.0, 2.0).astype(jnp.float32) / azimuth
    )
    cosine_part = jnp.dot(
        (jnp.cos(source_angle) * weights[:, None]).T,
        jnp.cos(target_angle),
        precision=lax.Precision.HIGHEST,
        preferred_element_type=jnp.float32,
    )
    sine_part = jnp.dot(
        (jnp.sin(source_angle) * weights[:, None]).T,
        jnp.sin(target_angle),
        precision=lax.Precision.HIGHEST,
        preferred_element_type=jnp.float32,
    )
    return cosine_part + sine_part


def phase_angle(level_num, first_row, row_count, polar_count, azimuth):
    polar_angle = (
        math.pi
        / polar_count
        * ((first_row + jnp.arange(row_count, dtype=jnp.int32)).astype(jnp.float32) + 0.5)
    )
    azimuth_angle = two_pi / azimuth * jnp.arange(azimuth, dtype=jnp.int32).astype(jnp.float32)
    pick_axis = (level_num - 1) % 3
    if pick_axis == 0:
        direction = jnp.sin(polar_angle)[:, None] * jnp.cos(azimuth_angle)[None, :]
    elif pick_axis == 1:
        direction = jnp.sin(polar_angle)[:, None] * jnp.sin(azimuth_angle)[None, :]
    else:
        direction = jnp.cos(polar_angle)[:, None] * jnp.ones((1, azimuth), jnp.float32)
    return step_phase * direction


def rotate(widened, rotation):
    cosine = jnp.cos(rotation)
    sine_part = jnp.sin(rotation)
    real_part = widened[..., 0, :]
    imag_part = widened[..., 1, :]
    return jnp.concatenate(
        [cosine * real_part - sine_part * imag_part, sine_part * real_part + cosine * imag_part],
        axis=-1,
    )


def shift_terms(block, rotation):
    half_span = block.shape[-1] // 2
    split_parts = block.reshape(block.shape[:-1] + (2, half_span))
    return rotate(split_parts, rotation)


def reflect_rows(block):
    half_span = block.shape[-1] // 2
    split_parts = block.reshape(block.shape[:-1] + (2, half_span))
    return jnp.roll(split_parts, half_span // 2, axis=-1).reshape(block.shape)


def polar_refine(extended):
    row_count = extended.shape[-2] - 4

    def rows_at(offset):
        return extended[..., offset : offset + row_count, :]

    even_rows = (
        outer_weight * rows_at(0)
        + inner_weight * rows_at(1)
        + center_weight * rows_at(2)
        + across_weight * rows_at(3)
    )
    odd_rows = (
        across_weight * rows_at(1)
        + center_weight * rows_at(2)
        + inner_weight * rows_at(3)
        + outer_weight * rows_at(4)
    )
    paired = jnp.stack([even_rows, odd_rows], axis=-2)
    return paired.reshape(extended.shape[:-2] + (2 * row_count, extended.shape[-1]))


def azimuth_refine(block, interp_matrix):
    half_span = block.shape[-1] // 2
    split_parts = block.reshape(block.shape[:-1] + (2, half_span))
    widened = jnp.einsum(
        "...cw,wv->...cv",
        split_parts,
        interp_matrix,
        precision=lax.Precision.HIGHEST,
        preferred_element_type=jnp.float32,
    )
    return widened.reshape(block.shape[:-1] + (4 * half_span,))


def translate(slab_data, far_rows, type_rows, operator_rows):
    box_total, row_count, sample_span = slab_data.shape
    far_count = far_rows.shape[1]
    type_total = operator_rows.shape[0]
    half_span = sample_span // 2
    flat_slab = slab_data.reshape(box_total, row_count * sample_span)
    flat_ops = operator_rows.reshape(type_total, row_count * sample_span)
    box_pick = (
        far_rows.reshape(-1)[:, None] == jnp.arange(box_total, dtype=jnp.int32)[None, :]
    ).astype(jnp.float32)
    type_pick = (
        type_rows.reshape(-1)[:, None] == jnp.arange(type_total, dtype=jnp.int32)[None, :]
    ).astype(jnp.bfloat16)
    chosen = jnp.dot(
        box_pick, flat_slab, precision=lax.Precision.HIGHEST, preferred_element_type=jnp.float32
    )
    operator_part = jnp.dot(type_pick, flat_ops, preferred_element_type=jnp.bfloat16)
    chosen = chosen.reshape(box_total, far_count, row_count, 2, half_span)
    operator_part = operator_part.reshape(box_total, far_count, row_count, 2, half_span).astype(
        jnp.float32
    )
    real_left = operator_part[..., 0, :]
    imag_left = operator_part[..., 1, :]
    real_right = chosen[..., 0, :]
    imag_right = chosen[..., 1, :]
    real_sum = jnp.sum(real_left * real_right - imag_left * imag_right, axis=1)
    imag_sum = jnp.sum(real_left * imag_right + imag_left * real_right, axis=1)
    return jnp.concatenate([real_sum, imag_sum], axis=-1)


def split_halves(merged, groups, side_bit):
    slot_count = merged.shape[0]
    halves = merged.reshape((groups, 2, slot_count // (2 * groups)) + merged.shape[1:])
    kept_half = lax.dynamic_index_in_dim(halves, side_bit, 1, keepdims=False).reshape(
        (slot_count // 2,) + merged.shape[1:]
    )
    given_half = lax.dynamic_index_in_dim(halves, 1 - side_bit, 1, keepdims=False).reshape(
        (slot_count // 2,) + merged.shape[1:]
    )
    return (kept_half, given_half)


def first_level(extended, groups, first_row):
    row_count = extended.shape[1] - 4
    azimuth = extended.shape[2] // 2
    interp_matrix = interp_table(azimuth)
    angle_rows = phase_angle(1, first_row, 2 * row_count, 2 * TH, 2 * azimuth)
    side_bit = lax.axis_index("dir") & 1
    flip_sign = 2.0 * side_bit.astype(jnp.float32) - 1.0
    refined = azimuth_refine(polar_refine(extended), interp_matrix)
    kept_half, given_half = split_halves(refined, groups, side_bit)
    arrived = swapped(shift_terms(given_half, flip_sign * angle_rows), "dir", 0)
    return shift_terms(kept_half, flip_sign * angle_rows) + arrived


def merge_level(merged, level_num, groups, first_row):
    row_count = merged.shape[1]
    azimuth = merged.shape[2] // 2
    angle_rows = phase_angle(level_num, first_row, row_count, 2 * TH, azimuth)
    side_bit = lax.axis_index("dir") >> level_num - 1 & 1
    flip_sign = 2.0 * side_bit.astype(jnp.float32) - 1.0
    kept_half, given_half = split_halves(merged, groups, side_bit)
    arrived = swapped(shift_terms(given_half, flip_sign * angle_rows), "dir", level_num - 1)
    return shift_terms(kept_half, flip_sign * angle_rows) + arrived


def shards(patterns, far_boxes, far_types, transfer):
    regrouped = lax.all_to_all(patterns, "box", split_axis=2, concat_axis=0, tiled=True)
    box_count, box_slots, row_count, sample_span = regrouped.shape
    slab_data = regrouped.reshape(box_count * box_slots, row_count, sample_span)
    incoming = translate(slab_data, far_boxes[0], far_types[0], transfer)[None]
    padded = extended_2(slab_data, (("box", 1),), 2)
    position = lax.axis_index("box")
    top_rows = jnp.where(position == 0, reflect_rows(slab_data[:, 0:2][:, ::-1]), padded[:, 0:2])
    bottom_rows = jnp.where(
        position == lax.axis_size("box") - 1,
        reflect_rows(slab_data[:, row_count - 2 :][:, ::-1]),
        padded[:, row_count + 2 :],
    )
    extended = jnp.concatenate([top_rows, padded[:, 2 : row_count + 2], bottom_rows], axis=1)
    first_row = position * (2 * row_count)
    merged = first_level(extended, box_count, first_row)
    for level_index in range(1, LEVELS):
        merged = merge_level(merged, level_index + 1, box_count, first_row)
    return (incoming, merged)


def solution(mesh):
    return jax.shard_map(
        shards,
        mesh=mesh,
        in_specs=(
            P("box", "dir", None, None),
            P("dir", None, None),
            P("dir", None, None),
            P(None, "box", None),
        ),
        out_specs=(P("dir", None, "box", None), P("dir", "box", None)),
        check_vma=False,
    )
```

profile of v0, /device:TPU:1, one launch (start us, length us, event | category | flops | bytes accessed | tf_op | source)
XLA Modules:
  0.0 144.7 jit_solution(16579372142956762281)
XLA Ops:
  0.6 2.1 %copy.53 = f32[1,8,64,256]{3,1,0,2:T(8,128)} copy(f32[1,8,64,256]{3,2,1,0:T(8,128)} %param.4) | data formatting | bytes 1048576 | tf_op args[0]
  2.8 17.6 %all-to-all-start = ((f32[1,8,64,256]{3,1,0,2:T(8,128)}), f32[1,8,64,256]{3,1,0,2:T(8,128)S(1)}, u32[]{:S(2)}, u32[]{:S(2)}) async-start(f32[1,8,64,256]{3,1,0,2:T(8,128)} %copy.53), calls=%async_computation | async-start | bytes 1048576 | tf_op jit(solution)/shard_map/all_to_all | solution.py:215
  20.4 0.7 fusion.34
  21.2 0.7 fusion.2
  21.9 0.3 fusion.54
  22.2 7.6 %all-to-all-done = f32[1,8,64,256]{3,1,0,2:T(8,128)S(1)} async-done(((f32[1,8,64,256]{3,1,0,2:T(8,128)}), f32[1,8,64,256]{3,1,0,2:T(8,128)S(1)}, u32[]{:S(2)}, u32[]{:S(2)}) %all-to-all-start) | async-done | bytes 524320 | tf_op jit(solution)/shard_map/all_to_all | solution.py:215
  29.8 0.2 copy.54
  30.1 0.2 rev.6
  30.4 2.8 %collective-permute-start.1 = (f32[32,2,256]{2,1,0:T(2,128)S(1)}, f32[32,2,256]{2,1,0:T(2,128)S(1)}, u32[]{:S(2)}, u32[]{:S(2)}) collective-permute-start(f32[32,2,256]{2,1,0:T(2,128)S(1)} %get-tuple-element.28), channel_id=1, source_target_pairs={{256,0},{512,256},{768,512},{257,1},{513,257},{769,513},{258,2},{5... | collective-permute-start | bytes 196616 | tf_op jit(solution)/shard_map/ppermute | solution.py:38
  33.2 0.2 rev.7
  33.4 4.5 %collective-permute-start = (f32[32,2,256]{2,1,0:T(2,128)S(1)}, f32[32,2,256]{2,1,0:T(2,128)S(1)}, u32[]{:S(2)}, u32[]{:S(2)}) collective-permute-start(f32[32,2,256]{2,1,0:T(2,128)S(1)} %get-tuple-element.29), channel_id=1, source_target_pairs={{0,256},{256,512},{512,768},{1,257},{257,513},{513,769},{2,258},{2... | collective-permute-start | bytes 196616 | tf_op jit(solution)/shard_map/ppermute | solution.py:37
  38.8 0.2 collective-permute-done
  39.0 0.5 fusion.13
  39.6 0.6 copy.58
  40.2 0.5 reshape_reshape.28
  40.7 2.2 %fusion.3 = f32[32,32,2,256]{3,1,2,0:T(8,128)S(1)} fusion(f32[128,256,1,1]{1,0,3,2:T(8,128)S(1)} %fusion.2, f32[32,32,2,128]{3,2,0,1:T(2,128)S(1)} %reshape_reshape.28), kind=kOutput, calls=%fused_computation.10 | convolution fusion | flops 805306368 | bytes 3276800 | tf_op jit(solution)/shard_map/...cw,wv->...cv/dot_general | solution.py:138
  42.9 3.0 %copy.60 = f32[32,32,2,256]{3,2,1,0:T(2,128)} copy(f32[32,32,2,256]{3,1,2,0:T(8,128)S(1)} %fusion.3) | data formatting | bytes 4194304 | tf_op jit(solution)/shard_map/...cw,wv->...cv/dot_general | solution.py:138
  45.9 2.9 %reshape_reshape.29 = f32[4,2,4,32,512]{4,3,2,1,0:T(8,128)S(1)} reshape(f32[32,32,2,256]{3,2,1,0:T(2,128)} %copy.60) | data formatting | bytes 4194304 | tf_op jit(solution)/shard_map/reshape;reshape | solution.py:180
  48.8 1.6 %constant_dynamic-slice_fusion.1 = (f32[4,1,4,32,512]{4,3,2,1,0:T(8,128)}, f32[4,1,4,32,512]{4,3,2,1,0:T(8,128)}) fusion(f32[4,2,4,32,512]{4,3,2,1,0:T(8,128)S(1)} %reshape_reshape.29, s32[]{:T(128)S(6)} %select_n.69, s32[]{:T(128)S(6)} %select_n.70), kind=kLoop, calls=%fused_computation.112 | loop fusion | bytes 4194312 | tf_op jit(solution)/shard_map/jit(dynamic_index_in_dim)/dynamic_slice | solution.py:181
  50.4 1.9 %reshape_reshape.30 = f32[16,32,2,256]{3,2,1,0:T(2,128)S(1)} reshape(f32[4,1,4,32,512]{4,3,2,1,0:T(8,128)} %get-tuple-element.4) | data formatting | bytes 2097152 | tf_op jit(solution)/shard_map/reshape;reshape | solution.py:103
  52.3 1.9 %reshape_reshape.31 = f32[16,32,2,256]{3,2,1,0:T(2,128)S(1)} reshape(f32[4,1,4,32,512]{4,3,2,1,0:T(8,128)} %get-tuple-element.5) | data formatting | bytes 2097152 | tf_op jit(solution)/shard_map/reshape;reshape | solution.py:103
  54.2 2.3 %fusion.79 = (f32[16,32,1,256]{3,2,1,0:T(1,128)S(1)}, f32[16,32,1,256]{3,2,1,0:T(1,128)S(1)}, f32[16,32,1,256]{3,2,1,0:T(1,128)S(1)}, f32[16,32,1,256]{3,2,1,0:T(1,128)S(1)}) fusion(f32[16,32,2,256]{3,2,1,0:T(2,128)S(1)} %reshape_reshape.30, f32[16,32,2,256]{3,2,1,0:T(2,128)S(1)} %reshape_reshape.31), kind=kLoop, calls=%fused_computation.137 | loop fusion | bytes 4194304 | tf_op jit(solution)/shard_map/slice | solution.py:94
  56.5 1.2 fusion.17
  57.8 1.1 pad_maximum_fusion.1
  58.9 2.1 %collective-permute-start.2 = (f32[16,32,512]{2,1,0:T(8,128)}, f32[16,32,512]{2,1,0:T(8,128)}, u32[]{:S(2)}, u32[]{:S(2)}) collective-permute-start(f32[16,32,512]{2,1,0:T(8,128)} %pad_maximum_fusion.1), channel_id=1, source_target_pairs={{0,1},{1,0},{2,3},{3,2},{4,5},{5,4},{6,7},{7,6},{8,9},{9,8},{10,11... | collective-permute-start | bytes 3145736 | tf_op jit(solution)/shard_map/ppermute | solution.py:27
  61.4 2.8 %copy.93 = bf16[40,8,16,256]{3,1,2,0:T(8,128)(2,1)} copy(bf16[40,8,16,256]{3,2,1,0:T(8,128)(2,1)S(1)} %bitcast.168) | data formatting | bytes 5242880
  64.1 6.1 %dot_general.24 = bf16[16,2,128,316]{2,1,0,3:T(2,128)(2,1)S(1)} reshape(bf16[4096,316]{0,1:T(8,128)(2,1)} %bitcast.169) | data formatting | bytes 5177344 | tf_op jit(solution)/shard_map/dot_general | solution.py:164
  70.3 5.7 %convolution_convert_fusion = f32[32,16,16,2,128]{4,1,3,2,0:T(8,128)} fusion(bf16[16,2,128,316]{2,1,0,3:T(2,128)(2,1)S(1)} %dot_general.24, s32[32,16]{1,0:T(8,128)S(1)} %copy.50), kind=kOutput, calls=%fused_computation.2 | convolution fusion | flops 1327659008 | bytes 10979328 | tf_op jit(solution)/shard_map/dot_general | solution.py:164
  76.0 8.4 %collective-permute-done.2 = f32[16,32,512]{2,1,0:T(8,128)} collective-permute-done((f32[16,32,512]{2,1,0:T(8,128)}, f32[16,32,512]{2,1,0:T(8,128)}, u32[]{:S(2)}, u32[]{:S(2)}) %collective-permute-start.2) | collective-permute-done | bytes 1048608 | tf_op jit(solution)/shard_map/ppermute | solution.py:27
  84.4 1.4 maximum_add_fusion
  85.9 0.3 reshape_reshape.32
  86.3 0.5 fusion.81
  86.8 0.3 reshape_reshape.33
  87.1 0.5 fusion.82
  87.8 0.9 pad_maximum_fusion.4
  88.7 1.9 %collective-permute-start.3 = (f32[8,32,512]{2,1,0:T(8,128)}, f32[8,32,512]{2,1,0:T(8,128)S(1)}, u32[]{:S(2)}, u32[]{:S(2)}) collective-permute-start(f32[8,32,512]{2,1,0:T(8,128)} %pad_maximum_fusion.4), channel_id=1, source_target_pairs={{0,2},{2,0},{1,3},{3,1},{4,6},{6,4},{5,7},{7,5},{8,10},{10,8},{9,1... | collective-permute-start | bytes 1572872 | tf_op jit(solution)/shard_map/ppermute | solution.py:27
  90.7 0.3 copy.94
  91.0 0.4 dot_general.27
  91.4 5.7 %fusion.19 = f32[32,16,16,2,128]{4,1,3,2,0:T(8,128)} fusion(f32[16,2,128,32]{2,1,0,3:T(2,128)S(1)} %dot_general.27, s32[32,16]{1,0:T(8,128)S(1)} %copy.52), kind=kOutput, calls=%fused_computation.40 | convolution fusion | flops 805322752 | bytes 8914944 | tf_op jit(solution)/shard_map/dot_general | solution.py:161
  97.1 18.3 %collective-permute-done.3 = f32[8,32,512]{2,1,0:T(8,128)S(1)} collective-permute-done((f32[8,32,512]{2,1,0:T(8,128)}, f32[8,32,512]{2,1,0:T(8,128)S(1)}, u32[]{:S(2)}, u32[]{:S(2)}) %collective-permute-start.3) | collective-permute-done | bytes 524320 | tf_op jit(solution)/shard_map/ppermute | solution.py:27
  115.6 0.2 reshape_reshape.34
  115.8 0.2 fusion.85
  116.1 0.2 fusion.86
  116.5 1.9 %collective-permute-start.4 = (f32[4,32,512]{2,1,0:T(8,128)S(1)}, f32[4,32,512]{2,1,0:T(8,128)S(1)}, u32[]{:S(2)}, u32[]{:S(2)}) collective-permute-start(f32[4,32,512]{2,1,0:T(8,128)S(1)} %pad_maximum_fusion.5), channel_id=1, source_target_pairs={{0,4},{4,0},{1,5},{5,1},{2,6},{6,2},{3,7},{7,3},{8,12},{12,8},{9,1... | collective-permute-start | bytes 786440 | tf_op jit(solution)/shard_map/ppermute | solution.py:27
  118.4 7.9 %subtract_reduce_fusion = (f32[32,16,128]{2,1,0:T(8,128)S(1)}, f32[32,16,128]{2,1,0:T(8,128)S(1)}) fusion(f32[32,16,16,2,128]{4,1,3,2,0:T(8,128)} %fusion.19, f32[32,16,16,2,128]{4,1,3,2,0:T(8,128)} %convolution_convert_fusion), kind=kLoop, calls=%fused_computation.1 | loop fusion | flops 8257536 | bytes 17301504 | tf_op jit(solution)/shard_map/reduce_sum | solution.py:173
  126.4 0.8 maximum_bitcast_fusion
  127.2 16.8 %collective-permute-done.4 = f32[4,32,512]{2,1,0:T(8,128)S(1)} collective-permute-done((f32[4,32,512]{2,1,0:T(8,128)S(1)}, f32[4,32,512]{2,1,0:T(8,128)S(1)}, u32[]{:S(2)}, u32[]{:S(2)}) %collective-permute-start.4) | collective-permute-done | bytes 262176 | tf_op jit(solution)/shard_map/ppermute | solution.py:27
  144.0 0.7 maximum_add_fusion.2
  (38 shorter events, 2.3 us)
Async XLA Ops:
  2.8 27.1 %all-to-all-start = ((f32[1,8,64,256]{3,1,0,2:T(8,128)}), f32[1,8,64,256]{3,1,0,2:T(8,128)S(1)}, u32[]{:S(2)}, u32[]{:S(2)}) async-start(f32[1,8,64,256]{3,1,0,2:T(8,128)} %copy.53), calls=%async_computation | async-start | bytes 1048576 | tf_op jit(solution)/shard_map/all_to_all | solution.py:215
  30.4 8.4 %collective-permute-start.1 = (f32[32,2,256]{2,1,0:T(2,128)S(1)}, f32[32,2,256]{2,1,0:T(2,128)S(1)}, u32[]{:S(2)}, u32[]{:S(2)}) collective-permute-start(f32[32,2,256]{2,1,0:T(2,128)S(1)} %get-tuple-element.28), channel_id=1, source_target_pairs={{256,0},{512,256},{768,512},{257,1},{513,257},{769,513},{258,2},{5... | collective-permute-start | bytes 196616 | tf_op jit(solution)/shard_map/ppermute | solution.py:38
  33.4 5.6 %collective-permute-start = (f32[32,2,256]{2,1,0:T(2,128)S(1)}, f32[32,2,256]{2,1,0:T(2,128)S(1)}, u32[]{:S(2)}, u32[]{:S(2)}) collective-permute-start(f32[32,2,256]{2,1,0:T(2,128)S(1)} %get-tuple-element.29), channel_id=1, source_target_pairs={{0,256},{256,512},{512,768},{1,257},{257,513},{513,769},{2,258},{2... | collective-permute-start | bytes 196616 | tf_op jit(solution)/shard_map/ppermute | solution.py:37
  56.5 4.5 %copy-start.3 = (s32[1,32,16]{1,2,0:T(8,128)S(1)}, s32[1,32,16]{1,2,0:T(8,128)}, u32[]{:S(2)}) copy-start(s32[1,32,16]{1,2,0:T(8,128)} %param.5) | copy-start | bytes 6148
  56.5 4.6 %copy-start.4 = (s32[1,32,16]{1,2,0:T(8,128)S(1)}, s32[1,32,16]{1,2,0:T(8,128)}, u32[]{:S(2)}) copy-start(s32[1,32,16]{1,2,0:T(8,128)} %param.6) | copy-start | bytes 6148
  56.5 4.7 %copy-start = (bf16[316,16,256]{2,1,0:T(8,128)(2,1)S(1)}, bf16[316,16,256]{2,1,0:T(8,128)(2,1)}, u32[]{:S(2)}) copy-start(bf16[316,16,256]{2,1,0:T(8,128)(2,1)} %param.7) | copy-start | bytes 7766020
  58.9 25.5 %collective-permute-start.2 = (f32[16,32,512]{2,1,0:T(8,128)}, f32[16,32,512]{2,1,0:T(8,128)}, u32[]{:S(2)}, u32[]{:S(2)}) collective-permute-start(f32[16,32,512]{2,1,0:T(8,128)} %pad_maximum_fusion.1), channel_id=1, source_target_pairs={{0,1},{1,0},{2,3},{3,2},{4,5},{5,4},{6,7},{7,6},{8,9},{9,8},{10,11... | collective-permute-start | bytes 3145736 | tf_op jit(solution)/shard_map/ppermute | solution.py:27
  70.3 14.1 %copy-start.1 = (f32[16,32,256]{2,1,0:T(8,128)S(1)}, f32[16,32,256]{2,1,0:T(8,128)}, u32[]{:S(2)}) copy-start(f32[16,32,256]{2,1,0:T(8,128)} %get-tuple-element.6) | copy-start | bytes 1572868
  70.3 14.1 %copy-start.2 = (f32[16,32,256]{2,1,0:T(8,128)S(1)}, f32[16,32,256]{2,1,0:T(8,128)}, u32[]{:S(2)}) copy-start(f32[16,32,256]{2,1,0:T(8,128)} %get-tuple-element.7) | copy-start | bytes 1572868
  88.7 26.8 %collective-permute-start.3 = (f32[8,32,512]{2,1,0:T(8,128)}, f32[8,32,512]{2,1,0:T(8,128)S(1)}, u32[]{:S(2)}, u32[]{:S(2)}) collective-permute-start(f32[8,32,512]{2,1,0:T(8,128)} %pad_maximum_fusion.4), channel_id=1, source_target_pairs={{0,2},{2,0},{1,3},{3,1},{4,6},{6,4},{5,7},{7,5},{8,10},{10,8},{9,1... | collective-permute-start | bytes 1572872 | tf_op jit(solution)/shard_map/ppermute | solution.py:27
  116.5 27.5 %collective-permute-start.4 = (f32[4,32,512]{2,1,0:T(8,128)S(1)}, f32[4,32,512]{2,1,0:T(8,128)S(1)}, u32[]{:S(2)}, u32[]{:S(2)}) collective-permute-start(f32[4,32,512]{2,1,0:T(8,128)S(1)} %pad_maximum_fusion.5), channel_id=1, source_target_pairs={{0,4},{4,0},{1,5},{5,1},{2,6},{6,2},{3,7},{7,3},{8,12},{12,8},{9,1... | collective-permute-start | bytes 786440 | tf_op jit(solution)/shard_map/ppermute | solution.py:27
where the time goes:
time: 145 us
  waiting for transfers between devices  51.4 us (35%)
  starting transfers between devices  30.8 us (21%)
  local copies, waits for them, and re-layouts  30.7 us (21%)
  other arithmetic  15.9 us (11%)
  matrix products  14.8 us (10%)
    ppermute x3, waiting for transfers between devices, swapped(): return lax.ppermute(block, axis, route)  43.5 us
    all_to_all x1, starting transfers between devices, shards(): lax.all_to_all(patterns, 'box', split_axis=2, concat_axis=0, tiled=True)  17.6 us
    reduce_sum x1, other arithmetic, translate(): real_sum = jnp.sum(real_left * real_right - imag_left * imag_right, axis=1)  7.91 us
    all_to_all x1, waiting for transfers between devices, shards(): lax.all_to_all(patterns, 'box', split_axis=2, concat_axis=0, tiled=True)  7.63 us
    dot_general x1, local copies, waits for them, and re-layouts, translate(): jnp.dot(type_pick, flat_ops, preferred_element_type=jnp.bfloat16)  6.15 us
    ppermute x3, starting transfers between devices, swapped(): return lax.ppermute(block, axis, route)  5.96 us
    dot_general x1, matrix products, translate(): jnp.dot(type_pick, flat_ops, preferred_element_type=jnp.bfloat16)  5.66 us
    dot_general x1, matrix products, translate(): jnp.dot(box_pick, flat_slab, precision=lax.Precision.HIGHEST, preferred_e...  5.66 us
  transfers between devices with their start and end apart: 6, of which 5 were waited for; matrix products, arithmetic and copies ran while one was open for 23% of the time, Pallas kernels for 0%

commit v1 on v0

v1 whole, which is shorter than its diff:
```python
import math

import jax
import jax.numpy as jnp
from jax import lax
from jax.experimental import pallas as pl
from jax.experimental.pallas import tpu as pltpu
from jax.sharding import PartitionSpec as P

MESH = pl.DeviceIdType.MESH
F32, BF16 = jnp.float32, jnp.bfloat16

TH, PHI, BOXES, FAR, GROUP, OCTET, N_BOX = 64, 128, 8, 16, 32, 8, 4
SLAB = TH // N_BOX
CHUNKS = 4
ROWS = (24, 16, 16, 8)
ASCENDING = (0, 24, 40, 56)
DESCENDING = (40, 24, 8, 0)

two_pi = 2.0 * math.pi
step_phase = 8.0
outer_weight = -0.0390625
inner_weight = 0.2734375
center_weight = 0.8203125
across_weight = -0.0546875


def halves(value):
    high = value.astype(BF16)
    return high, (value - high.astype(F32)).astype(BF16)


def index_like(shape, dim):
    return lax.broadcasted_iota(jnp.int32, shape, dim)


def interp_tables(high_ref, low_ref):
    shape = (PHI, 2 * PHI)
    apart = 2 * index_like(shape, 0) - index_like(shape, 1)
    odd = lax.rem(apart + 2 * PHI, 2) == 1
    sign = jnp.where(lax.rem(apart + 2 * PHI, 4) == 1, 1.0, -1.0)
    angle = (math.pi / (2 * PHI)) * apart.astype(F32)
    value = sign * jnp.cos(angle) / (PHI * jnp.where(odd, jnp.sin(angle), 1.0))
    value = jnp.where(odd, value, jnp.where(apart == 0, 1.0, 0.0))
    high, low = halves(value)
    high_ref[0:PHI] = high
    high_ref[PHI : 2 * PHI] = high
    low_ref[...] = low


def phase_tables(signs, lateral, axial):
    shape = (2 * TH, 2 * PHI)
    polar = (math.pi / (2 * TH)) * (index_like(shape, 0).astype(F32) + 0.5)
    azimuth = (two_pi / (2 * PHI)) * index_like(shape, 1).astype(F32)
    sine = step_phase * jnp.sin(polar)
    first, second = sine * jnp.cos(azimuth), sine * jnp.sin(azimuth)
    cos_1, sin_1 = jnp.cos(first), signs[0] * jnp.sin(first)
    cos_2, sin_2 = jnp.cos(second), signs[1] * jnp.sin(second)
    lateral[0] = cos_1 * cos_2
    lateral[1] = sin_1 * cos_2
    lateral[2] = cos_1 * sin_2
    lateral[3] = sin_1 * sin_2
    third = step_phase * jnp.cos(polar)
    axial[0] = jnp.cos(third)
    axial[1] = signs[2] * jnp.sin(third)


def polar_weights(slab):
    shape = (2 * SLAB, 4 * SLAB)
    row, column = index_like(shape, 0), lax.rem(index_like(shape, 1), 2 * SLAB)
    column = jnp.where((slab == 0) & (column < 8), 7 - column, column)
    column = jnp.where((slab == N_BOX - 1) & (column >= 24), 55 - column, column)
    offset = column - 8 - row // 2
    flipped = jnp.where(lax.rem(row, 2) == 0, offset, -offset)
    weights = jnp.zeros(shape, F32)
    for place, weight in ((-2, outer_weight), (-1, inner_weight), (0, center_weight), (1, across_weight)):
        weights = jnp.where(flipped == place, weight, weights)
    return weights.astype(BF16)


def kernel(
    pat, far_boxes, far_types, transfer, incoming, aggregated,
    ext, slab, ops, inc, made, kept, fb, ft, high, low, lateral, axial,
    z_send, z_recv, x_send, x_recv, a_send, a_recv, local,
):
    q, r = lax.axis_index("box"), lax.axis_index("dir")
    l = lax.rem(r, OCTET)
    base = r - l
    bits = (lax.rem(l, 2), lax.rem(l // 2, 2), l // 4)
    upper, core = q // 2, lax.rem(q, 2)

    def sibling(d):
        n = [b if not d >> s & 1 else 1 - b for s, b in enumerate(bits)]
        return base + n[0] + 2 * n[1] + 4 * n[2], 4 * n[0] + 2 * n[1] + n[2]

    def box_peer(e):
        c = 1 - core if e & 1 else core
        u = 1 - upper if e & 2 else upper
        return 2 * u + c

    barrier = pltpu.get_barrier_semaphore()
    for d in range(1, OCTET):
        pl.semaphore_signal(barrier, inc=1, device_id=(q, sibling(d)[0]), device_id_type=MESH)
    for e in range(1, N_BOX):
        pl.semaphore_signal(barrier, inc=1, device_id=(box_peer(e), r), device_id_type=MESH)

    locals_ = [
        pltpu.make_async_copy(far_boxes.at[0], fb, local.at[0]),
        pltpu.make_async_copy(far_types.at[0], ft, local.at[1]),
        pltpu.make_async_copy(transfer, ops, local.at[2]),
        pltpu.make_async_copy(pat.at[0, sibling(0)[1]], ext.at[0, pl.ds(8, TH)], local.at[3]),
        pltpu.make_async_copy(
            pat.at[0, :, pl.ds(pl.multiple_of(SLAB * q, 8), SLAB)],
            slab.at[pl.ds(BOXES * q, BOXES)],
            local.at[4],
        ),
    ]
    for copy in locals_:
        copy.start()
    pl.semaphore_wait(barrier, OCTET - 1 + N_BOX - 1)

    def z_copy(c, d):
        other, box = sibling(d)
        first = pl.multiple_of(upper * ASCENDING[c] + (1 - upper) * DESCENDING[c], 8)
        return pltpu.make_async_remote_copy(
            src_ref=pat.at[0, box, pl.ds(first, ROWS[c])],
            dst_ref=ext.at[d, pl.ds(pl.multiple_of(8 + first, 8), ROWS[c])],
            send_sem=z_send.at[c, d],
            recv_sem=z_recv.at[c, d],
            device_id=(q, other),
            device_id_type=MESH,
        )

    def x_copy(e):
        other = box_peer(e)
        return pltpu.make_async_remote_copy(
            src_ref=pat.at[0, :, pl.ds(pl.multiple_of(SLAB * other, 8), SLAB)],
            dst_ref=slab.at[pl.ds(BOXES * q, BOXES)],
            send_sem=x_send.at[e],
            recv_sem=x_recv.at[e],
            device_id=(other, r),
            device_id_type=MESH,
        )

    def a_copy(c):
        target = upper * c + (1 - upper) * (N_BOX - 1 - c)
        return pltpu.make_async_remote_copy(
            src_ref=made.at[c],
            dst_ref=kept.at[q],
            send_sem=a_send.at[c],
            recv_sem=a_recv.at[q],
            device_id=(target, r),
            device_id_type=MESH,
        )

    order = (7, 6, 5, 4, 3, 2, 1)
    z_copies = [[z_copy(c, d) for d in order] for c in range(CHUNKS)]
    x_copies = [x_copy(e) for e in (3, 2, 1)]
    for copy in z_copies[0] + x_copies + z_copies[1] + z_copies[2] + z_copies[3]:
        copy.start()

    signs = [2.0 * b.astype(F32) - 1.0 for b in bits]
    interp_tables(high, low)
    phase_tables(signs, lateral, axial)

    def translation():
        for copy in (locals_[0], locals_[1], locals_[2], locals_[4]):
            copy.wait()
        for copy in x_copies:
            copy.wait_recv()

        def one_box(g, carry):
            real = jnp.zeros((SLAB, PHI), F32)
            imag = jnp.zeros((SLAB, PHI), F32)
            for k in range(FAR):
                box, kind = fb[g, k], ft[g, k]
                value = slab[box]
                factor = ops[kind].astype(F32)
                value_r, value_i = value[:, :PHI], value[:, PHI:]
                factor_r, factor_i = factor[:, :PHI], factor[:, PHI:]
                real += factor_r * value_r - factor_i * value_i
                imag += factor_r * value_i + factor_i * value_r
            inc[g, :, 0:PHI] = real
            inc[g, :, PHI : 2 * PHI] = imag
            return carry

        lax.fori_loop(0, GROUP, one_box, 0)
        out = pltpu.make_async_copy(inc, incoming.at[0], local.at[5])
        out.start()
        return out

    def refine(c):
        target = upper * c + (1 - upper) * (N_BOX - 1 - c)
        if c in (0, CHUNKS - 1):
            bottom = 1 - upper if c == 0 else upper
            source = pl.multiple_of(8 + bottom * (TH - 8), 8)
            place = pl.multiple_of(bottom * (TH + 8), 8)
            for d in range(OCTET):
                rows = ext[d, pl.ds(source, 8), :]
                ext[d, pl.ds(place, 8), 0:PHI] = pltpu.roll(rows[:, :PHI], PHI // 2, 1)
                ext[d, pl.ds(place, 8), PHI : 2 * PHI] = pltpu.roll(rows[:, PHI:], PHI // 2, 1)
        window = pl.ds(pl.multiple_of(SLAB * target, 8), 2 * SLAB)
        sums = [ext[d, window, :] for d in range(OCTET)]
        for s in (1, 2, 4):
            sums = [sums[k] + sums[k ^ s] if not k & s else sums[k ^ s] - sums[k] for k in range(OCTET)]
        weights = polar_weights(target)
        rows = []
        for k in range(OCTET):
            pieces = jnp.concatenate(halves(sums[k]), axis=0)
            polar = jnp.dot(weights, pieces, preferred_element_type=F32)
            rows += [polar[:, :PHI], polar[:, PHI:]]
        stacked_high, stacked_low = halves(jnp.concatenate(rows, axis=0))
        both = jnp.concatenate([stacked_high, stacked_low], axis=1)
        wide = jnp.dot(both, high[...], preferred_element_type=F32)
        wide += jnp.dot(stacked_high, low[...], preferred_element_type=F32)
        angles = pl.ds(pl.multiple_of(2 * SLAB * target, 8), 2 * SLAB)
        parts = []
        for third in range(2):
            real, imag = 0.0, 0.0
            for k in range(4):
                at = 4 * SLAB * (4 * third + k)
                w_r = wide[at : at + 2 * SLAB]
                w_i = wide[at + 2 * SLAB : at + 4 * SLAB]
                table = lateral[k, angles, :]
                if k == 0:
                    real, imag = table * w_r, table * w_i
                elif k == 3:
                    real, imag = real - table * w_r, imag - table * w_i
                else:
                    real, imag = real - table * w_i, imag + table * w_r
            parts.append((real, imag))
        cosine, sine = axial[0, angles, :], axial[1, angles, :]
        made[c, :, 0 : 2 * PHI] = cosine * parts[0][0] - sine * parts[1][1]
        made[c, :, 2 * PHI : 4 * PHI] = cosine * parts[0][1] + sine * parts[1][0]

        @pl.when(target != q)
        def _():
            a_copy(c).start()

        @pl.when(target == q)
        def _():
            kept[q] = made[c]

    locals_[3].wait()
    inc_out = None
    for c in range(CHUNKS):
        for copy in z_copies[c]:
            copy.wait_recv()
        refine(c)
        if c == 1:
            inc_out = translation()

    for e in range(1, N_BOX):
        other = box_peer(e)
        pltpu.make_async_remote_copy(
            src_ref=made.at[0],
            dst_ref=kept.at[other],
            send_sem=a_send.at[0],
            recv_sem=a_recv.at[other],
            device_id=(other, r),
            device_id_type=MESH,
        ).wait_recv()
    agg_out = pltpu.make_async_copy(kept, aggregated, local.at[6])
    agg_out.start()
    for c in range(CHUNKS):
        target = upper * c + (1 - upper) * (N_BOX - 1 - c)

        @pl.when(target != q)
        def _():
            a_copy(c).wait_send()

        for copy in z_copies[c]:
            copy.wait_send()
    for copy in x_copies:
        copy.wait_send()
    inc_out.wait()
    agg_out.wait()


def shards(patterns, far_boxes, far_types, transfer):
    anywhere = pl.BlockSpec(memory_space=pl.ANY)
    vmem = pltpu.VMEM
    dma = pltpu.SemaphoreType.DMA
    return pl.pallas_call(
        kernel,
        out_shape=(
            jax.ShapeDtypeStruct((1, GROUP, SLAB, 2 * PHI), F32),
            jax.ShapeDtypeStruct((N_BOX, 2 * SLAB, 4 * PHI), F32),
        ),
        in_specs=[anywhere] * 4,
        out_specs=(anywhere, anywhere),
        scratch_shapes=[
            vmem((OCTET, TH + 16, 2 * PHI), F32),
            vmem((GROUP, SLAB, 2 * PHI), F32),
            vmem(transfer.shape, BF16),
            vmem((GROUP, SLAB, 2 * PHI), F32),
            vmem((CHUNKS, 2 * SLAB, 4 * PHI), F32),
            vmem((N_BOX, 2 * SLAB, 4 * PHI), F32),
            pltpu.SMEM((GROUP, FAR), jnp.int32),
            pltpu.SMEM((GROUP, FAR), jnp.int32),
            vmem((2 * PHI, 2 * PHI), BF16),
            vmem((PHI, 2 * PHI), BF16),
            vmem((4, 2 * TH, 2 * PHI), F32),
            vmem((2, 2 * TH, 2 * PHI), F32),
            dma((CHUNKS, OCTET)),
            dma((CHUNKS, OCTET)),
            dma((N_BOX,)),
            dma((N_BOX,)),
            dma((CHUNKS,)),
            dma((N_BOX,)),
            dma((7,)),
        ],
        compiler_params=pltpu.CompilerParams(
            collective_id=0, has_side_effects=True, vmem_limit_bytes=48 * 1024 * 1024
        ),
    )(patterns, far_boxes, far_types, transfer)


def solution(mesh):
    return jax.shard_map(
        shards,
        mesh=mesh,
        in_specs=(
            P("box", "dir", None, None),
            P("dir", None, None),
            P("dir", None, None),
            P(None, "box", None),
        ),
        out_specs=(P("dir", None, "box", None), P("dir", "box", None)),
        check_vma=False,
    )
```

time: 145 us -> 46.9 us (0.32)
  waiting for transfers between devices: 51.4 us -> 0 us
  Pallas kernels: 0 us -> 40.2 us
  starting transfers between devices: 30.8 us -> 0 us
  local copies, waits for them, and re-layouts: 30.7 us -> 5.81 us
  other arithmetic: 15.9 us -> 0 us
  matrix products: 14.8 us -> 0 us
    ppermute x5 -> x0, waiting for transfers between devices: 43.7 us -> none  [the longest x3 43.5 us: swapped(): return lax.ppermute(block, axis, route)]
    pallas_call x0 -> x1, Pallas kernels: none -> 40.2 us  [shards(): pl.pallas_call(kernel, out_shape=(jax.ShapeDtypeStruct((1, GROUP, SLAB, 2...]
    all_to_all x1 -> x0, starting transfers between devices: 17.6 us -> none  [shards(): lax.all_to_all(patterns, 'box', split_axis=2, concat_axis=0, tiled=True)]
    dot_general x5 -> x0, matrix products: 14.8 us -> none  [the longest x1 5.66 us: translate(): jnp.dot(type_pick, flat_ops, preferred_element_type=jnp.bfloat16)]
    ppermute x5 -> x0, starting transfers between devices: 13.2 us -> none  [the longest x3 5.96 us: swapped(): return lax.ppermute(block, axis, route)]
    dot_general x3 -> x0, local copies, waits for them, and re-layouts: 9.58 us -> none  [the longest x1 6.15 us: translate(): jnp.dot(type_pick, flat_ops, preferred_element_type=jnp.bfloat16)]
    another operation x9 -> x0, local copies, waits for them, and re-layouts: 8.86 us -> none  [the longest x6 4.77 us: shift_terms(): split_parts = block.reshape(block.shape[:-1] + (2, half_span))]
    reduce_sum x1 -> x0, other arithmetic: 7.91 us -> none  [translate(): real_sum = jnp.sum(real_left * real_right - imag_left * imag_right, axis=1)]
  transfers between devices with their start and end apart: 6 -> 0, of which waited for: 5 -> 0; matrix products, arithmetic and copies ran while one was open for 23% -> 0% of each run, Pallas kernels for 0% -> 0%
where the time goes in v1:
time: 46.9 us; the launch traced here: 46.6 us
  Pallas kernels  40.2 us (86%)
  local copies, waits for them, and re-layouts  5.81 us (12%)
  between operations  0.64 us (1%)
    pallas_call x1, Pallas kernels, shards(): pl.pallas_call(kernel, out_shape=(jax.ShapeDtypeStruct((1, GROUP, SLAB, 2...  40.2 us
    unnamed x8, local copies, waits for them, and re-layouts  5.81 us

profile of v1, /device:TPU:1, one launch (start us, length us, event | category | flops | bytes accessed | tf_op | source)
XLA Modules:
  0.0 46.6 jit_solution(2466984704037110739)
XLA Ops:
  0.6 0.8 %copy.6.far_boxes = s32[1,32,16]{2,1,0:T(8,128)S(1)} copy(s32[1,32,16]{1,2,0:T(8,128)} %param.5) | data formatting | bytes 4096 | tf_op args[1]
  1.4 0.8 %copy.7.far_types = s32[1,32,16]{2,1,0:T(8,128)S(1)} copy(s32[1,32,16]{1,2,0:T(8,128)} %param.6) | data formatting | bytes 4096 | tf_op args[2]
  2.2 0.0 copy-start
  2.2 1.7 %copy-done = bf16[316,16,256]{2,1,0:T(8,128)(2,1)S(1)} copy-done((bf16[316,16,256]{2,1,0:T(8,128)(2,1)S(1)}, bf16[316,16,256]{2,1,0:T(8,128)(2,1)}, u32[]{:S(2)}) %copy-start) | copy-done | bytes 2588696
  3.9 0.0 copy-start.1
  3.9 1.0 %copy-done.1 = f32[1,8,64,256]{3,2,1,0:T(8,128)S(1)} copy-done((f32[1,8,64,256]{3,2,1,0:T(8,128)S(1)}, f32[1,8,64,256]{3,2,1,0:T(8,128)}, u32[]{:S(2)}) %copy-start.1) | copy-done | bytes 524312
  4.9 40.2 %shard_map.59 = (f32[1,32,16,256]{3,2,1,0:T(8,128)S(1)}, f32[4,32,512]{2,1,0:T(8,128)S(1)}) custom-call(f32[1,8,64,256]{3,2,1,0:T(8,128)S(1)} %copy-done.1, s32[1,32,16]{2,1,0:T(8,128)S(1)} %copy.6.far_boxes, s32[1,32,16]{2,1,0:T(8,128)S(1)} %copy.7.far_types, bf16[316,16,256]{2,1,0:T(8,128)(2,1)S(1)} %copy-done), custom_call_target="tpu_custom_call" | custom-call | tf_op jit(solution)/shard_map/pallas_call | solution.py:284
  45.1 0.8 %copy.10 = f32[1,32,16,256]{3,2,1,0:T(8,128)} copy(f32[1,32,16,256]{3,2,1,0:T(8,128)S(1)} %get-tuple-element.4) | data formatting | bytes 1048576
  45.9 0.7 %copy.11 = f32[4,32,512]{2,1,0:T(8,128)} copy(f32[4,32,512]{2,1,0:T(8,128)S(1)} %get-tuple-element.5) | data formatting | bytes 524288
Async XLA Ops:
  2.2 1.7 %copy-start = (bf16[316,16,256]{2,1,0:T(8,128)(2,1)S(1)}, bf16[316,16,256]{2,1,0:T(8,128)(2,1)}, u32[]{:S(2)}) copy-start(bf16[316,16,256]{2,1,0:T(8,128)(2,1)} %transfer.1) | copy-start | bytes 7766020
  3.9 1.0 %copy-start.1 = (f32[1,8,64,256]{3,2,1,0:T(8,128)S(1)}, f32[1,8,64,256]{3,2,1,0:T(8,128)}, u32[]{:S(2)}) copy-start(f32[1,8,64,256]{3,2,1,0:T(8,128)} %pat.1) | copy-start | bytes 1572868

commit v2 on v1

--- a/solution.py
+++ b/solution.py
@@ -48,21 +48,21 @@
     low_ref[...] = low
 
 
-def phase_tables(signs, lateral, axial):
+def phase_tables(lateral, axial):
     shape = (2 * TH, 2 * PHI)
     polar = (math.pi / (2 * TH)) * (index_like(shape, 0).astype(F32) + 0.5)
     azimuth = (two_pi / (2 * PHI)) * index_like(shape, 1).astype(F32)
     sine = step_phase * jnp.sin(polar)
     first, second = sine * jnp.cos(azimuth), sine * jnp.sin(azimuth)
-    cos_1, sin_1 = jnp.cos(first), signs[0] * jnp.sin(first)
-    cos_2, sin_2 = jnp.cos(second), signs[1] * jnp.sin(second)
+    cos_1, sin_1 = jnp.cos(first), jnp.sin(first)
+    cos_2, sin_2 = jnp.cos(second), jnp.sin(second)
     lateral[0] = cos_1 * cos_2
     lateral[1] = sin_1 * cos_2
     lateral[2] = cos_1 * sin_2
     lateral[3] = sin_1 * sin_2
     third = step_phase * jnp.cos(polar)
     axial[0] = jnp.cos(third)
-    axial[1] = signs[2] * jnp.sin(third)
+    axial[1] = jnp.sin(third)
 
 
 def polar_weights(slab):
@@ -79,36 +79,59 @@
 
 
 def kernel(
-    pat, far_boxes, far_types, transfer, incoming, aggregated,
-    ext, slab, ops, inc, made, kept, fb, ft, high, low, lateral, axial,
-    z_send, z_recv, x_send, x_recv, a_send, a_recv, local,
+    pat, far_boxes, far_types, transfer, incoming, kept,
+    ext, slab, ops, made, fb, ft, high, low, lateral, axial,
+    known, known_box, z_send, z_recv, x_send, x_recv, a_send, a_recv, local,
 ):
     q, r = lax.axis_index("box"), lax.axis_index("dir")
-    l = lax.rem(r, OCTET)
-    base = r - l
-    bits = (lax.rem(l, 2), lax.rem(l // 2, 2), l // 4)
+    place = lax.rem(r, OCTET)
+    base = r - place
     upper, core = q // 2, lax.rem(q, 2)
 
-    def sibling(d):
-        n = [b if not d >> s & 1 else 1 - b for s, b in enumerate(bits)]
-        return base + n[0] + 2 * n[1] + 4 * n[2], 4 * n[0] + 2 * n[1] + n[2]
+    def kept_box(p):
+        return 4 * lax.rem(p, 2) + 2 * lax.rem(p // 2, 2) + p // 4
 
     def box_peer(e):
         c = 1 - core if e & 1 else core
         u = 1 - upper if e & 2 else upper
         return 2 * u + c
 
+    def tell(semaphore, p):
+        pl.semaphore_signal(semaphore, inc=1, device_id=(q, base + p), device_id_type=MESH)
+
     barrier = pltpu.get_barrier_semaphore()
-    for d in range(1, OCTET):
-        pl.semaphore_signal(barrier, inc=1, device_id=(q, sibling(d)[0]), device_id_type=MESH)
-    for e in range(1, N_BOX):
-        pl.semaphore_signal(barrier, inc=1, device_id=(box_peer(e), r), device_id_type=MESH)
+
+    staggered = lax.rem(r // OCTET, 4) < 2
+    together = jnp.logical_not(staggered)
+    rank = lax.rem(place + OCTET - 1, OCTET)
+    ranked = [(p, (p + OCTET - 1) % OCTET) for p in (1, 2, 3, 4, 5, 6, 7, 0)]
+
+    for p, other in ranked:
+
+        @pl.when((other > rank) | (together & (other < rank)))
+        def _():
+            tell(barrier, p)
+
+    def tell_box(semaphore, other):
+        pl.semaphore_signal(semaphore, inc=1, device_id=(other, r), device_id_type=MESH)
+
+    for b in range(N_BOX - 1):
+
+        @pl.when(b < q)
+        def _():
+            tell_box(barrier, b)
+
+    for b in range(1, N_BOX):
+
+        @pl.when(together & (b > q))
+        def _():
+            tell_box(barrier, b)
 
     locals_ = [
         pltpu.make_async_copy(far_boxes.at[0], fb, local.at[0]),
         pltpu.make_async_copy(far_types.at[0], ft, local.at[1]),
         pltpu.make_async_copy(transfer, ops, local.at[2]),
-        pltpu.make_async_copy(pat.at[0, sibling(0)[1]], ext.at[0, pl.ds(8, TH)], local.at[3]),
+        pltpu.make_async_copy(pat.at[0, kept_box(place)], ext.at[place, pl.ds(8, TH)], local.at[3]),
         pltpu.make_async_copy(
             pat.at[0, :, pl.ds(pl.multiple_of(SLAB * q, 8), SLAB)],
             slab.at[pl.ds(BOXES * q, BOXES)],
@@ -117,28 +140,63 @@
     ]
     for copy in locals_:
         copy.start()
-    pl.semaphore_wait(barrier, OCTET - 1 + N_BOX - 1)
-
-    def z_copy(c, d):
-        other, box = sibling(d)
+    expected = jnp.where(together, OCTET - 1 + N_BOX - 1, rank + N_BOX - 1 - q)
+
+    @pl.when(expected > 0)
+    def _():
+        pl.semaphore_wait(barrier, expected)
+
+    for p, other in ranked:
+
+        @pl.when(staggered & (other < rank))
+        def _():
+            tell(known.at[place], p)
+
+    for b in range(1, N_BOX):
+
+        @pl.when(staggered & (b > q))
+        def _():
+            tell_box(known_box.at[q], b)
+
+    def z_copy(c, p):
         first = pl.multiple_of(upper * ASCENDING[c] + (1 - upper) * DESCENDING[c], 8)
         return pltpu.make_async_remote_copy(
-            src_ref=pat.at[0, box, pl.ds(first, ROWS[c])],
-            dst_ref=ext.at[d, pl.ds(pl.multiple_of(8 + first, 8), ROWS[c])],
-            send_sem=z_send.at[c, d],
-            recv_sem=z_recv.at[c, d],
-            device_id=(q, other),
+            src_ref=pat.at[0, kept_box(p), pl.ds(first, ROWS[c])],
+            dst_ref=ext.at[place, pl.ds(pl.multiple_of(8 + first, 8), ROWS[c])],
+            send_sem=z_send.at[c, p],
+            recv_sem=z_recv.at[c, place],
+            device_id=(q, base + p),
             device_id_type=MESH,
         )
 
-    def x_copy(e):
-        other = box_peer(e)
+    def z_arrival(c, p):
+        first = pl.multiple_of(upper * ASCENDING[c] + (1 - upper) * DESCENDING[c], 8)
         return pltpu.make_async_remote_copy(
-            src_ref=pat.at[0, :, pl.ds(pl.multiple_of(SLAB * other, 8), SLAB)],
+            src_ref=pat.at[0, 0, pl.ds(first, ROWS[c])],
+            dst_ref=ext.at[p, pl.ds(pl.multiple_of(8 + first, 8), ROWS[c])],
+            send_sem=z_send.at[c, p],
+            recv_sem=z_recv.at[c, p],
+            device_id=(q, base + p),
+            device_id_type=MESH,
+        )
+
+    def x_copy(b):
+        return pltpu.make_async_remote_copy(
+            src_ref=pat.at[0, :, pl.ds(SLAB * b, SLAB)],
             dst_ref=slab.at[pl.ds(BOXES * q, BOXES)],
-            send_sem=x_send.at[e],
-            recv_sem=x_recv.at[e],
-            device_id=(other, r),
+            send_sem=x_send.at[b],
+            recv_sem=x_recv.at[q],
+            device_id=(b, r),
+            device_id_type=MESH,
+        )
+
+    def x_arrival(b):
+        return pltpu.make_async_remote_copy(
+            src_ref=pat.at[0, :, pl.ds(SLAB * b, SLAB)],
+            dst_ref=slab.at[pl.ds(BOXES * b, BOXES)],
+            send_sem=x_send.at[b],
+            recv_sem=x_recv.at[b],
+            device_id=(b, r),
             device_id_type=MESH,
         )
 
@@ -153,41 +211,88 @@
             device_id_type=MESH,
         )
 
-    order = (7, 6, 5, 4, 3, 2, 1)
-    z_copies = [[z_copy(c, d) for d in order] for c in range(CHUNKS)]
-    x_copies = [x_copy(e) for e in (3, 2, 1)]
-    for copy in z_copies[0] + x_copies + z_copies[1] + z_copies[2] + z_copies[3]:
-        copy.start()
-
-    signs = [2.0 * b.astype(F32) - 1.0 for b in bits]
+    def meet(p):
+        @pl.when(staggered)
+        def _():
+            pl.semaphore_wait(known.at[p], 1)
+
+    for distance in range(1, OCTET):
+
+        @pl.when((place > distance) | (place == 0))
+        def _():
+            z_copy(0, jnp.where(place == 0, distance, place - distance)).start()
+
+    for b in range(1, N_BOX):
+
+        @pl.when(b > q)
+        def _():
+            x_copy(b).start()
+
+    for distance in range(1, OCTET):
+
+        @pl.when((place > 0) & (place + distance < OCTET))
+        def _():
+            meet(place + distance)
+            z_copy(0, place + distance).start()
+
+    for p in range(1, OCTET):
+
+        @pl.when(p != place)
+        def _():
+            z_copy(1, p).start()
+
+    @pl.when(place > 0)
+    def _():
+        meet(0)
+        z_copy(0, 0).start()
+        z_copy(1, 0).start()
+
+    for b in range(N_BOX - 1):
+
+        @pl.when(b < q)
+        def _():
+            @pl.when(staggered)
+            def _():
+                pl.semaphore_wait(known_box.at[b], 1)
+
+            x_copy(b).start()
+
+    for c in range(2, CHUNKS):
+        for p in range(OCTET):
+
+            @pl.when(p != place)
+            def _():
+                z_copy(c, p).start()
+
     interp_tables(high, low)
-    phase_tables(signs, lateral, axial)
+    phase_tables(lateral, axial)
 
     def translation():
         for copy in (locals_[0], locals_[1], locals_[2], locals_[4]):
             copy.wait()
-        for copy in x_copies:
-            copy.wait_recv()
+        for b in range(N_BOX):
+
+            @pl.when(b != q)
+            def _():
+                x_arrival(b).wait_recv()
+
 
         def one_box(g, carry):
             real = jnp.zeros((SLAB, PHI), F32)
             imag = jnp.zeros((SLAB, PHI), F32)
             for k in range(FAR):
-                box, kind = fb[g, k], ft[g, k]
+                box, kind = fb[k, g], ft[k, g]
                 value = slab[box]
                 factor = ops[kind].astype(F32)
                 value_r, value_i = value[:, :PHI], value[:, PHI:]
                 factor_r, factor_i = factor[:, :PHI], factor[:, PHI:]
                 real += factor_r * value_r - factor_i * value_i
                 imag += factor_r * value_i + factor_i * value_r
-            inc[g, :, 0:PHI] = real
-            inc[g, :, PHI : 2 * PHI] = imag
+            incoming[0, g, :, 0:PHI] = real
+            incoming[0, g, :, PHI : 2 * PHI] = imag
             return carry
 
         lax.fori_loop(0, GROUP, one_box, 0)
-        out = pltpu.make_async_copy(inc, incoming.at[0], local.at[5])
-        out.start()
-        return out
 
     def refine(c):
         target = upper * c + (1 - upper) * (N_BOX - 1 - c)
@@ -202,7 +307,7 @@
         window = pl.ds(pl.multiple_of(SLAB * target, 8), 2 * SLAB)
         sums = [ext[d, window, :] for d in range(OCTET)]
         for s in (1, 2, 4):
-            sums = [sums[k] + sums[k ^ s] if not k & s else sums[k ^ s] - sums[k] for k in range(OCTET)]
+            sums = [sums[k] + sums[k ^ s] if not k & s else sums[k] - sums[k ^ s] for k in range(OCTET)]
         weights = polar_weights(target)
         rows = []
         for k in range(OCTET):
@@ -242,13 +347,16 @@
             kept[q] = made[c]
 
     locals_[3].wait()
-    inc_out = None
     for c in range(CHUNKS):
-        for copy in z_copies[c]:
-            copy.wait_recv()
+        for p in range(OCTET):
+
+            @pl.when(p != place)
+            def _():
+                z_arrival(c, p).wait_recv()
+
         refine(c)
         if c == 1:
-            inc_out = translation()
+            translation()
 
     for e in range(1, N_BOX):
         other = box_peer(e)
@@ -260,8 +368,6 @@
             device_id=(other, r),
             device_id_type=MESH,
         ).wait_recv()
-    agg_out = pltpu.make_async_copy(kept, aggregated, local.at[6])
-    agg_out.start()
     for c in range(CHUNKS):
         target = upper * c + (1 - upper) * (N_BOX - 1 - c)
 
@@ -269,51 +375,56 @@
         def _():
             a_copy(c).wait_send()
 
-        for copy in z_copies[c]:
-            copy.wait_send()
-    for copy in x_copies:
-        copy.wait_send()
-    inc_out.wait()
-    agg_out.wait()
+        for p in range(OCTET):
+
+            @pl.when(p != place)
+            def _():
+                z_copy(c, p).wait_send()
+
+    for b in range(N_BOX):
+
+        @pl.when(b != q)
+        def _():
+            x_copy(b).wait_send()
 
 
 def shards(patterns, far_boxes, far_types, transfer):
-    anywhere = pl.BlockSpec(memory_space=pl.ANY)
+    anywhere = pl.BlockSpec(memory_space=pltpu.HBM)
     vmem = pltpu.VMEM
     dma = pltpu.SemaphoreType.DMA
     return pl.pallas_call(
         kernel,
         out_shape=(
-            jax.ShapeDtypeStruct((1, GROUP, SLAB, 2 * PHI), F32),
-            jax.ShapeDtypeStruct((N_BOX, 2 * SLAB, 4 * PHI), F32),
+            pltpu.VMEM((1, GROUP, SLAB, 2 * PHI), F32),
+            pltpu.VMEM((N_BOX, 2 * SLAB, 4 * PHI), F32),
         ),
         in_specs=[anywhere] * 4,
-        out_specs=(anywhere, anywhere),
+        out_specs=(pl.BlockSpec(memory_space=vmem),) * 2,
         scratch_shapes=[
             vmem((OCTET, TH + 16, 2 * PHI), F32),
             vmem((GROUP, SLAB, 2 * PHI), F32),
             vmem(transfer.shape, BF16),
-            vmem((GROUP, SLAB, 2 * PHI), F32),
             vmem((CHUNKS, 2 * SLAB, 4 * PHI), F32),
-            vmem((N_BOX, 2 * SLAB, 4 * PHI), F32),
-            pltpu.SMEM((GROUP, FAR), jnp.int32),
-            pltpu.SMEM((GROUP, FAR), jnp.int32),
+            pltpu.SMEM((FAR, GROUP), jnp.int32),
+            pltpu.SMEM((FAR, GROUP), jnp.int32),
             vmem((2 * PHI, 2 * PHI), BF16),
             vmem((PHI, 2 * PHI), BF16),
             vmem((4, 2 * TH, 2 * PHI), F32),
             vmem((2, 2 * TH, 2 * PHI), F32),
+            pltpu.SemaphoreType.REGULAR((OCTET,)),
+            pltpu.SemaphoreType.REGULAR((N_BOX,)),
             dma((CHUNKS, OCTET)),
             dma((CHUNKS, OCTET)),
             dma((N_BOX,)),
             dma((N_BOX,)),
             dma((CHUNKS,)),
             dma((N_BOX,)),
-            dma((7,)),
+            dma((5,)),
         ],
         compiler_params=pltpu.CompilerParams(
-            collective_id=0, has_side_effects=True, vmem_limit_bytes=48 * 1024 * 1024
+            collective_id=0, has_side_effects=True, vmem_limit_bytes=56 * 1024 * 1024
         ),
-    )(patterns, far_boxes, far_types, transfer)
+    )(patterns, jnp.swapaxes(far_boxes, 1, 2), jnp.swapaxes(far_types, 1, 2), transfer)
 
 
 def solution(mesh):

time: 46.9 us -> 41.4 us (0.88)
  local copies, waits for them, and re-layouts: 5.81 us -> 1.5 us
  Pallas kernels: 40.2 us -> 39.1 us
    unnamed x8 -> x2, local copies, waits for them, and re-layouts: 5.81 us -> 1.5 us
    pallas_call x1, Pallas kernels: 40.2 us -> 39.1 us  [shards(): pl.pallas_call(kernel, out_shape=(pltpu.VMEM((1, GROUP, SLAB, 2 * PHI), F...]
where the time goes in v2:
time: 41.4 us; the launch traced here: 41.2 us
  Pallas kernels  39.1 us (94%)
  local copies, waits for them, and re-layouts  1.5 us (4%)
  between operations  0.64 us (2%)
    pallas_call x1, Pallas kernels, shards(): pl.pallas_call(kernel, out_shape=(pltpu.VMEM((1, GROUP, SLAB, 2 * PHI), F...  39.1 us
    unnamed x2, local copies, waits for them, and re-layouts  1.5 us

profile of v2, /device:TPU:1, one launch (start us, length us, event | category | flops | bytes accessed | tf_op | source)
XLA Modules:
  0.0 41.2 jit_solution(3751511678840175638)
XLA Ops:
  0.6 39.1 %shard_map.59 = (f32[1,32,16,256]{3,2,1,0:T(8,128)S(1)}, f32[4,32,512]{2,1,0:T(8,128)S(1)}) custom-call(f32[1,8,64,256]{3,2,1,0:T(8,128)} %pat.1, s32[1,16,32]{2,1,0:T(8,128)} %bitcast.2, s32[1,16,32]{2,1,0:T(8,128)} %bitcast.3, bf16[316,16,256]{2,1,0:T(8,128)(2,1)} %transfer.1), custom_call_target="tpu_custom_call" | custom-call | tf_op jit(solution)/shard_map/pallas_call | solution.py:395
  39.7 0.8 %copy.8 = f32[1,32,16,256]{3,2,1,0:T(8,128)} copy(f32[1,32,16,256]{3,2,1,0:T(8,128)S(1)} %get-tuple-element.2) | data formatting | bytes 1048576
  40.5 0.7 %copy.9 = f32[4,32,512]{2,1,0:T(8,128)} copy(f32[4,32,512]{2,1,0:T(8,128)S(1)} %get-tuple-element.3) | data formatting | bytes 524288

commit v3 on v2

--- a/solution.py
+++ b/solution.py
@@ -103,8 +103,10 @@
 
     staggered = lax.rem(r // OCTET, 4) < 2
     together = jnp.logical_not(staggered)
-    rank = lax.rem(place + OCTET - 1, OCTET)
-    ranked = [(p, (p + OCTET - 1) % OCTET) for p in (1, 2, 3, 4, 5, 6, 7, 0)]
+    turned = ((q == 0) & (r < OCTET)).astype(jnp.int32)
+    latest = (q == 0) & (r == 0)
+    rank = lax.rem(place + turned * (OCTET - 1), OCTET)
+    ranked = [(p, lax.rem(p + turned * (OCTET - 1), OCTET)) for p in range(OCTET)]
 
     for p, other in ranked:
 
@@ -115,15 +117,9 @@
     def tell_box(semaphore, other):
         pl.semaphore_signal(semaphore, inc=1, device_id=(other, r), device_id_type=MESH)
 
-    for b in range(N_BOX - 1):
-
-        @pl.when(b < q)
-        def _():
-            tell_box(barrier, b)
-
-    for b in range(1, N_BOX):
-
-        @pl.when(together & (b > q))
+    for b in range(N_BOX):
+
+        @pl.when((b > q) | (together & (b < q)))
         def _():
             tell_box(barrier, b)
 
@@ -138,9 +134,7 @@
             local.at[4],
         ),
     ]
-    for copy in locals_:
-        copy.start()
-    expected = jnp.where(together, OCTET - 1 + N_BOX - 1, rank + N_BOX - 1 - q)
+    expected = jnp.where(together, OCTET - 1 + N_BOX - 1, rank + q)
 
     @pl.when(expected > 0)
     def _():
@@ -152,9 +146,9 @@
         def _():
             tell(known.at[place], p)
 
-    for b in range(1, N_BOX):
-
-        @pl.when(staggered & (b > q))
+    for b in range(N_BOX - 1):
+
+        @pl.when(staggered & (b < q))
         def _():
             tell_box(known_box.at[q], b)
 
@@ -217,52 +211,68 @@
             pl.semaphore_wait(known.at[p], 1)
 
     for distance in range(1, OCTET):
-
-        @pl.when((place > distance) | (place == 0))
-        def _():
-            z_copy(0, jnp.where(place == 0, distance, place - distance)).start()
-
-    for b in range(1, N_BOX):
-
-        @pl.when(b > q)
+        lower = rank >= distance
+
+        @pl.when(lower)
+        def _():
+            z_copy(0, lax.rem(rank - distance + turned, OCTET)).start()
+
+    for copy in locals_:
+        copy.start()
+
+    for b in range(N_BOX - 1):
+
+        @pl.when(b < q)
         def _():
             x_copy(b).start()
 
     for distance in range(1, OCTET):
-
-        @pl.when((place > 0) & (place + distance < OCTET))
+        higher = rank + distance < OCTET - turned
+
+        @pl.when(higher)
         def _():
             meet(place + distance)
             z_copy(0, place + distance).start()
 
-    for p in range(1, OCTET):
-
-        @pl.when(p != place)
+    for b in range(1, N_BOX):
+
+        @pl.when(b > q)
+        def _():
+            @pl.when(staggered)
+            def _():
+                pl.semaphore_wait(known_box.at[b], 1)
+
+            x_copy(b).start()
+
+    for p in range(OCTET):
+
+        @pl.when((p != place) & ((p > 0) | (turned == 0) | (place == 0)))
         def _():
             z_copy(1, p).start()
 
-    @pl.when(place > 0)
+    @pl.when((turned == 1) & (place > 0))
     def _():
         meet(0)
-        z_copy(0, 0).start()
-        z_copy(1, 0).start()
-
-    for b in range(N_BOX - 1):
-
-        @pl.when(b < q)
-        def _():
-            @pl.when(staggered)
-            def _():
-                pl.semaphore_wait(known_box.at[b], 1)
-
-            x_copy(b).start()
-
-    for c in range(2, CHUNKS):
+        for c in range(2):
+            z_copy(c, 0).start()
+
+    @pl.when(together)
+    def _():
+        for c in range(2, CHUNKS):
+            for p in range(OCTET):
+
+                @pl.when(p != place)
+                def _():
+                    z_copy(c, p).start()
+
+    @pl.when(staggered)
+    def _():
         for p in range(OCTET):
 
             @pl.when(p != place)
             def _():
-                z_copy(c, p).start()
+                for c in range(2, CHUNKS):
+                    z_copy(c, p).start()
 
     interp_tables(high, low)
     phase_tables(lateral, axial)
@@ -356,7 +366,14 @@
 
         refine(c)
         if c == 1:
-            translation()
+
+            @pl.when(jnp.logical_not(latest))
+            def _():
+                translation()
+
+    @pl.when(latest)
+    def _():
+        translation()
 
     for e in range(1, N_BOX):
         other = box_peer(e)

time: 41.4 us -> 37.5 us (0.906); the launches traced: 41.2 us -> 36.9 us
  Pallas kernels: 39.1 us -> 34.7 us
    pallas_call x1, Pallas kernels: 39.1 us -> 34.7 us  [shards(): pl.pallas_call(kernel, out_shape=(pltpu.VMEM((1, GROUP, SLAB, 2 * PHI), F...]
where the time goes in v3:
time: 37.5 us; the launch traced here: 36.9 us
  Pallas kernels  34.7 us (93%)
  local copies, waits for them, and re-layouts  1.5 us (4%)
  between operations  0.64 us (2%)
    pallas_call x1, Pallas kernels, shards(): pl.pallas_call(kernel, out_shape=(pltpu.VMEM((1, GROUP, SLAB, 2 * PHI), F...  34.7 us
    unnamed x2, local copies, waits for them, and re-layouts  1.5 us

profile of v3, /device:TPU:1, one launch (start us, length us, event | category | flops | bytes accessed | tf_op | source)
XLA Modules:
  0.0 36.9 jit_solution(701638274719716258)
XLA Ops:
  0.6 34.7 %shard_map.59 = (f32[1,32,16,256]{3,2,1,0:T(8,128)S(1)}, f32[4,32,512]{2,1,0:T(8,128)S(1)}) custom-call(f32[1,8,64,256]{3,2,1,0:T(8,128)} %pat.1, s32[1,16,32]{2,1,0:T(8,128)} %bitcast.2, s32[1,16,32]{2,1,0:T(8,128)} %bitcast.3, bf16[316,16,256]{2,1,0:T(8,128)(2,1)} %transfer.1), custom_call_target="tpu_custom_call" | custom-call | tf_op jit(solution)/shard_map/pallas_call | solution.py:412
  35.4 0.8 %copy.8 = f32[1,32,16,256]{3,2,1,0:T(8,128)} copy(f32[1,32,16,256]{3,2,1,0:T(8,128)S(1)} %get-tuple-element.2) | data formatting | bytes 1048576
  36.2 0.7 %copy.9 = f32[4,32,512]{2,1,0:T(8,128)} copy(f32[4,32,512]{2,1,0:T(8,128)S(1)} %get-tuple-element.3) | data formatting | bytes 524288

commit v4 on v3

--- a/solution.py
+++ b/solution.py
@@ -405,11 +405,22 @@
             x_copy(b).wait_send()
 
 
+def finish(made_inc, made_agg, incoming, aggregated, sems):
+    copies = [
+        pltpu.make_async_copy(made_inc, incoming, sems.at[0]),
+        pltpu.make_async_copy(made_agg, aggregated, sems.at[1]),
+    ]
+    for copy in copies:
+        copy.start()
+    for copy in copies:
+        copy.wait()
+
+
 def shards(patterns, far_boxes, far_types, transfer):
     anywhere = pl.BlockSpec(memory_space=pltpu.HBM)
     vmem = pltpu.VMEM
     dma = pltpu.SemaphoreType.DMA
-    return pl.pallas_call(
+    results = pl.pallas_call(
         kernel,
         out_shape=(
             pltpu.VMEM((1, GROUP, SLAB, 2 * PHI), F32),
@@ -442,6 +453,14 @@
             collective_id=0, has_side_effects=True, vmem_limit_bytes=56 * 1024 * 1024
         ),
     )(patterns, jnp.swapaxes(far_boxes, 1, 2), jnp.swapaxes(far_types, 1, 2), transfer)
+    return pl.pallas_call(
+        finish,
+        out_shape=tuple(pltpu.HBM(v.shape, v.dtype) for v in results),
+        in_specs=[pl.BlockSpec(memory_space=pl.ANY)] * 2,
+        out_specs=(pl.BlockSpec(memory_space=pl.ANY),) * 2,
+        scratch_shapes=[dma((2,))],
+        compiler_params=pltpu.CompilerParams(vmem_limit_bytes=1024 * 1024),
+    )(*results)
 
 
 def solution(mesh):

time: 37.5 us -> 36.9 us (0.984)
  local copies, waits for them, and re-layouts: 1.5 us -> 0 us
  Pallas kernels: 34.7 us -> 35.6 us
    unnamed x2 -> x0, local copies, waits for them, and re-layouts: 1.5 us -> none
    pallas_call x0 -> x1, Pallas kernels: none -> 0.89 us  [shards(): pl.pallas_call(finish, out_shape=tuple((pltpu.HBM(v.shape, v.dtype) for v...]
where the time goes in v4:
time: 36.9 us; the launch traced here: 36.3 us
  Pallas kernels  35.6 us (96%)
  between operations  0.64 us (2%)
    pallas_call x1, Pallas kernels, shards(): pl.pallas_call(kernel, out_shape=(pltpu.VMEM((1, GROUP, SLAB, 2 * PHI), F...  34.7 us
    pallas_call x1, Pallas kernels, shards(): pl.pallas_call(finish, out_shape=tuple((pltpu.HBM(v.shape, v.dtype) for v...  0.89 us

profile of v4, /device:TPU:1, one launch (start us, length us, event | category | flops | bytes accessed | tf_op | source)
XLA Modules:
  0.0 36.3 jit_solution(8357274891992665029)
XLA Ops:
  0.6 34.7 %shard_map.59 = (f32[1,32,16,256]{3,2,1,0:T(8,128)S(1)}, f32[4,32,512]{2,1,0:T(8,128)S(1)}) custom-call(f32[1,8,64,256]{3,2,1,0:T(8,128)} %pat.1, s32[1,16,32]{2,1,0:T(8,128)} %bitcast.2, s32[1,16,32]{2,1,0:T(8,128)} %bitcast.3, bf16[316,16,256]{2,1,0:T(8,128)(2,1)} %transfer.1), custom_call_target="tpu_custom_call" | custom-call | tf_op jit(solution)/shard_map/pallas_call | solution.py:423
  35.4 0.9 %shard_map.60 = (f32[1,32,16,256]{3,2,1,0:T(8,128)}, f32[4,32,512]{2,1,0:T(8,128)}) custom-call(f32[1,32,16,256]{3,2,1,0:T(8,128)S(1)} %get-tuple-element.4.made_inc, f32[4,32,512]{2,1,0:T(8,128)S(1)} %get-tuple-element.5.made_agg), custom_call_target="tpu_custom_call" | custom-call | tf_op jit(solution)/shard_map/pallas_call | solution.py:456

commit v5 on v4

--- a/solution.py
+++ b/solution.py
@@ -265,13 +265,22 @@
                 def _():
                     z_copy(c, p).start()
 
-    @pl.when(staggered)
+    @pl.when(staggered & (place >= OCTET // 2))
     def _():
         for p in range(OCTET):
 
             @pl.when(p != place)
             def _():
                 for c in range(2, CHUNKS):
+                    z_copy(c, p).start()
+
+    @pl.when(staggered & (place < OCTET // 2))
+    def _():
+        for c in range(2, CHUNKS):
+            for p in (4, 5, 6, 7, 0, 1, 2, 3):
+
+                @pl.when(p != place)
+                def _():
                     z_copy(c, p).start()
 
     interp_tables(high, low)

time: 36.9 us -> 36.9 us (level)
  no operation moved by 1% of the time
where the time goes in v5:
time: 36.9 us; the launch traced here: 36.3 us
  Pallas kernels  35.6 us (96%)
  between operations  0.64 us (2%)
    pallas_call x1, Pallas kernels, shards(): pl.pallas_call(kernel, out_shape=(pltpu.VMEM((1, GROUP, SLAB, 2 * PHI), F...  34.7 us
    pallas_call x1, Pallas kernels, shards(): pl.pallas_call(finish, out_shape=tuple((pltpu.HBM(v.shape, v.dtype) for v...  0.89 us

profile of v5, /device:TPU:1, one launch (start us, length us, event | category | flops | bytes accessed | tf_op | source)
XLA Modules:
  0.0 36.3 jit_solution(11058056212510053913)
XLA Ops:
  0.6 34.7 %shard_map.59 = (f32[1,32,16,256]{3,2,1,0:T(8,128)S(1)}, f32[4,32,512]{2,1,0:T(8,128)S(1)}) custom-call(f32[1,8,64,256]{3,2,1,0:T(8,128)} %pat.1, s32[1,16,32]{2,1,0:T(8,128)} %bitcast.2, s32[1,16,32]{2,1,0:T(8,128)} %bitcast.3, bf16[316,16,256]{2,1,0:T(8,128)(2,1)} %transfer.1), custom_call_target="tpu_custom_call" | custom-call | tf_op jit(solution)/shard_map/pallas_call | solution.py:432
  35.4 0.9 %shard_map.60 = (f32[1,32,16,256]{3,2,1,0:T(8,128)}, f32[4,32,512]{2,1,0:T(8,128)}) custom-call(f32[1,32,16,256]{3,2,1,0:T(8,128)S(1)} %get-tuple-element.4.made_inc, f32[4,32,512]{2,1,0:T(8,128)S(1)} %get-tuple-element.5.made_agg), custom_call_target="tpu_custom_call" | custom-call | tf_op jit(solution)/shard_map/pallas_call | solution.py:465
